TPU v7x, 512 devices: a whole 4x8x8 slice. The times are simulated.
512 devices in a mesh: seq: 16 (over y, core), dp: 32 (over z, x).
Axes of the slice: x: 4, y: 8, z: 8, core: 2. Of those that a mesh axis runs over, the one named last changes fastest.
Arguments:
- latents: bfloat16 [64, 48, 128, 1152], P('dp', 'seq'), parts along dimension 0, may hold values from -6 to 6
- modulation: float32 [64, 3, 1152], P('dp'), parts along dimension 0, may hold values from -4 to 4
- w_qkv: bfloat16 [1152, 1728], P(None, 'seq'), may hold values from -0.1875 to 0.1875
- w_out: bfloat16 [576, 1152], P('seq'), may hold values from -0.25 to 0.25
- clip_frames: int32 [64], P('dp'), parts along dimension 0, may hold values from 12 to 48, as said below
- time_positions: int32 [64, 48], P('dp'), parts along dimension 0, may hold values from 0 to 204, as said below
Outputs:
- updated: bfloat16 [64, 48, 128, 1152], P('dp', 'seq'), parts along dimension 0
There are 32 independent parts, one for each index of `dp`. A program takes and returns all parts, laid end to end along the dimension named above; an argument that names none is the same for every part. Nothing has to cross between parts.
Inputs may be any that keep to these rules, and one draw needn't show every extreme that they name: Frames 0 to clip_frames - 1 of a clip hold data; at least 12 of them; some clip of every group has all 48. `time_positions`: within a clip the positions rise by 1 to 3 from each frame slot to the next; in every group some clip starts at 0 and some clip ends at 204.
All inputs are finite; a program needn't handle non-finite values.
Results may differ from a plain program's by a relative error of at most 0.0035.
Values may be sent and summed in bfloat16 or wider, within the bound.
A program may use at most 64 MiB of HBM per device.

v0:
```python
import math

import jax
import jax.numpy as jnp
from jax import lax
from jax.sharding import PartitionSpec as P

H = 8
HD = 72


def modulate(latents, modulation):
    values = latents.astype(jnp.float32)
    mean = jnp.mean(values, axis=-1, keepdims=True)
    var = jnp.mean((values - mean) ** 2, axis=-1, keepdims=True)
    normed = (values - mean) * lax.rsqrt(var + 1e-06)
    shift = modulation[:, 0][:, None, None, :]
    scale = modulation[:, 1][:, None, None, :]
    return (normed * (1.0 + scale) + shift).astype(jnp.bfloat16)


def rms_norm(vec):
    return vec * lax.rsqrt(jnp.mean(vec * vec, axis=-1, keepdims=True) + 1e-06)


def rotate(vec, angle):
    pairs = vec.reshape(vec.shape[:-1] + (HD // 2, 2))
    first = pairs[..., 0]
    second = pairs[..., 1]
    cosine = jnp.cos(angle)
    sine = jnp.sin(angle)
    turned = jnp.stack([first * cosine - second * sine, first * sine + second * cosine], axis=-1)
    return turned.reshape(vec.shape)


def attend(qkv, clip_frames, time_positions):
    clips, frames, patches, width = qkv.shape
    parts = qkv.reshape(clips, frames, patches, 3, H, HD)
    index = jnp.arange(HD // 2).astype(jnp.float32)
    freq = jnp.exp(-math.log(10000.0) * 2.0 * index / HD)
    angle = time_positions.astype(jnp.float32)[:, :, None, None, None] * freq
    query = rotate(rms_norm(parts[:, :, :, 0].astype(jnp.float32)), angle).astype(jnp.bfloat16)
    keys = rotate(rms_norm(parts[:, :, :, 1].astype(jnp.float32)), angle).astype(jnp.bfloat16)
    values = parts[:, :, :, 2]
    scores = jnp.einsum("btphd,bsphd->bphts", query, keys, preferred_element_type=jnp.float32)
    scores = scores * (1.0 / math.sqrt(HD))
    live = jnp.arange(frames)[None, :] < clip_frames[:, None]
    expo = jnp.where(live[:, None, None, None, :], jnp.exp(scores), 0.0)
    weights = (expo / jnp.sum(expo, axis=-1, keepdims=True)).astype(jnp.bfloat16)
    attended = jnp.einsum("bphts,bsphd->btphd", weights, values, preferred_element_type=jnp.float32)
    return attended.astype(jnp.bfloat16).reshape(clips, frames, patches, H * HD)


def shards(latents, modulation, w_qkv, w_out, clip_frames, time_positions):
    clips, local_frames, patches, width = latents.shape
    modulated = modulate(latents, modulation)
    flat = modulated.reshape(-1, width)
    joined = jnp.dot(
        flat, lax.all_gather(w_qkv, "seq", axis=1, tiled=True), preferred_element_type=jnp.float32
    )
    qkv = joined.astype(jnp.bfloat16).reshape(modulated.shape[:-1] + (joined.shape[-1],))
    qkv = lax.all_to_all(qkv, "seq", split_axis=2, concat_axis=1, tiled=True)
    attended = attend(qkv, clip_frames, time_positions)
    returned = lax.all_to_all(attended, "seq", split_axis=1, concat_axis=2, tiled=True)
    flat_out = returned.reshape(-1, returned.shape[-1])
    projected = jnp.dot(
        flat_out,
        lax.all_gather(w_out, "seq", axis=0, tiled=True),
        preferred_element_type=jnp.float32,
    )
    frame_ids = lax.axis_index("seq") * local_frames + jnp.arange(local_frames)
    live = (frame_ids[None, :] < clip_frames[:, None]).astype(jnp.float32)
    gate = modulation[:, 2][:, None, None, :]
    result = latents.astype(jnp.float32) + live[:, :, None, None] * gate * projected.reshape(
        clips, local_frames, patches, width
    )
    return result.astype(jnp.bfloat16)


def solution(mesh):
    return jax.shard_map(
        shards,
        mesh=mesh,
        in_specs=(
            P("dp", "seq", None, None),
            P("dp", None, None),
            P(None, "seq"),
            P("seq", None),
            P("dp"),
            P("dp", None),
        ),
        out_specs=P("dp", "seq", None, None),
        check_vma=False,
    )
```

profile of v0, /device:TPU:1, one launch (start us, length us, event | category | flops | bytes accessed | tf_op | source)
XLA Modules:
  0.0 248.6 jit_solution(10582361957653244125)
XLA Ops:
  6.5 0.0 copy-start.1
  6.5 0.0 copy-start.4
  6.5 0.0 all-gather.5.cloned.1.call-start
  6.5 0.7 all-gather.5.cloned.1.call-update
  7.3 1.8 convert_reduce_fusion
  9.1 0.0 copy-done.1
  9.1 0.6 fusion.2
  9.7 0.0 copy-done.4
  9.7 0.7 fusion.5
  10.5 49.5 %all-gather.5.cloned.1.call-done = bf16[16,108,1152]{2,1,0:T(8,128)(2,1)} async-done(((bf16[1,108,1152]{2,1,0:T(8,128)(2,1)}), bf16[16,108,1152]{2,1,0:T(8,128)(2,1)}) %all-gather.5.cloned.1.call-update) | async-done | bytes 3981328 | tf_op jit(solution)/shard_map/all_gather | solution.py:59
  59.9 4.9 %reshape.152 = bf16[1728,1152]{1,0:T(8,128)(2,1)} reshape(bf16[16,108,1152]{2,1,0:T(8,128)(2,1)} %all-gather.5.cloned.1.call-done) | data formatting | bytes 7962624
  64.8 7.3 %convolution_convert_fusion = bf16[768,1728]{0,1:T(8,128)(2,1)} fusion(bf16[768,1152]{1,0:T(8,128)(2,1)S(1)} %bitcast.51, bf16[1728,1152]{1,0:T(8,128)(2,1)} %reshape.152), kind=kOutput, calls=%fused_computation.11 | convolution fusion | flops 3058974720 | bytes 8404992 | tf_op jit(solution)/shard_map/dot_general | solution.py:58
  72.1 4.6 %copy.53 = bf16[768,1728]{1,0:T(8,128)(2,1)} copy(bf16[768,1728]{0,1:T(8,128)(2,1)} %convolution_convert_fusion) | data formatting | bytes 5308416 | tf_op jit(solution)/shard_map/convert_element_type | solution.py:61
  76.7 6.1 %copy.54 = bf16[2,3,128,1728]{3,0,1,2:T(2,128)(2,1)} copy(bf16[2,3,128,1728]{3,2,1,0:T(8,128)(2,1)} %bitcast.47) | data formatting | bytes 5308416 | tf_op jit(solution)/shard_map/reshape | solution.py:61
  82.8 0.0 copy-start.5
  82.8 0.0 copy-start.6
  82.8 4.6 %all-to-all-start = ((bf16[2,3,128,1728]{3,0,1,2:T(2,128)(2,1)}), bf16[2,3,128,1728]{3,0,1,2:T(2,128)(2,1)}, u32[]{:S(2)}, u32[]{:S(2)}) async-start(bf16[2,3,128,1728]{3,0,1,2:T(2,128)(2,1)} %copy.54), calls=%async_computation | async-start | bytes 5505024 | tf_op jit(solution)/shard_map/all_to_all | solution.py:62
  87.4 0.0 all-gather.7.cloned.1.call-start
  87.4 0.7 all-gather.7.cloned.1.call-update
  88.2 0.0 copy-done.5
  88.2 0.0 copy-done.6
  88.2 0.7 iota_compare_fusion
  88.9 0.9 multiply_cosine_fusion
  89.7 67.3 %all-to-all-done = bf16[2,3,128,1728]{3,0,1,2:T(2,128)(2,1)} async-done(((bf16[2,3,128,1728]{3,0,1,2:T(2,128)(2,1)}), bf16[2,3,128,1728]{3,0,1,2:T(2,128)(2,1)}, u32[]{:S(2)}, u32[]{:S(2)}) %all-to-all-start) | async-done | bytes 2654240 | tf_op jit(solution)/shard_map/all_to_all | solution.py:62
  157.1 2.0 copy.94
  159.1 1.8 copy.56
  160.9 8.8 %reshape.147 = bf16[2,48,8,3,8,72]{5,4,3,2,1,0:T(8,128)(2,1)} reshape(bf16[2,16,3,8,1728]{4,3,2,1,0:T(8,128)(2,1)} %copy.56) | data formatting | bytes 5308416 | tf_op jit(solution)/shard_map/reshape | solution.py:38
  169.7 4.5 %multiply_reduce_fusion.1 = (f32[2,48,8,8]{3,2,1,0:T(8,128)}, f32[2,48,8,8]{3,2,1,0:T(8,128)}) fusion(bf16[2,48,8,3,8,72]{5,4,3,2,1,0:T(8,128)(2,1)} %reshape.147), kind=kLoop, calls=%fused_computation.15 | loop fusion | flops 2641920 | bytes 1818624 | tf_op jit(solution)/shard_map/reduce_sum | solution.py:23
  174.2 6.2 %fusion.18 = (bf16[2,48,8,1,8,72]{5,4,3,2,1,0:T(8,128)(2,1)S(1)}, f32[2,48,8,1,8,72]{5,4,3,2,1,0:T(8,128)}, f32[2,48,8,1,8,72]{5,4,3,2,1,0:T(8,128)}) fusion(bf16[2,48,8,3,8,72]{5,4,3,2,1,0:T(8,128)(2,1)} %reshape.147), kind=kLoop, calls=%fused_computation.54 | loop fusion | flops 884736 | bytes 7077888 | tf_op jit(solution)/shard_map/slice | solution.py:44
  180.4 1.1 copy.59
  181.5 1.1 copy.61
  182.7 5.2 %copy.60 = f32[2,48,8,1,8,72]{1,4,5,2,0,3:T(8,128)} copy(f32[2,48,8,1,8,72]{5,4,3,2,1,0:T(8,128)} %get-tuple-element.12) | data formatting | bytes 3538944 | tf_op jit(solution)/shard_map/convert_element_type | solution.py:43
  187.9 5.2 %copy.58 = f32[2,48,8,1,8,72]{1,4,5,2,0,3:T(8,128)} copy(f32[2,48,8,1,8,72]{5,4,3,2,1,0:T(8,128)} %get-tuple-element.13) | data formatting | bytes 3538944 | tf_op jit(solution)/shard_map/convert_element_type | solution.py:42
  193.1 0.0 copy-start
  193.1 2.8 %broadcast_multiply_fusion = f32[2,48,8,8,36,2]{1,3,5,4,2,0:T(8,128)S(1)} fusion(f32[2,48,8,8,36,2]{1,3,5,4,2,0:T(8,128)} %bitcast.46, f32[2,48,8,8]{1,3,2,0:T(8,128)S(1)} %add_rsqrt_fusion), kind=kLoop, calls=%fused_computation.25 | loop fusion | flops 442368 | bytes 3563520 | tf_op jit(solution)/shard_map/mul | solution.py:23
  196.0 0.9 copy-done
  196.9 0.0 copy-start.2
  196.9 0.0 copy-start.3
  196.9 0.4 broadcast_multiply_fusion.1
  197.3 0.4 copy-done.2
  197.7 0.0 copy-done.3
  197.7 1.3 subtract_convert_fusion.1
  198.9 0.0 copy-start.7
  198.9 1.1 pad_maximum_fusion
  200.1 0.0 copy-done.7
  200.1 1.2 fusion.7
  201.3 1.9 fusion.12
  203.2 0.4 copy.73
  203.6 2.0 reshape.156
  205.6 5.4 %all-to-all-start.1 = ((bf16[2,48,8,576]{3,2,0,1:T(8,128)(2,1)}), bf16[2,48,8,576]{3,2,0,1:T(8,128)(2,1)}, u32[]{:S(2)}, u32[]{:S(2)}) async-start(bf16[2,48,8,576]{3,2,0,1:T(8,128)(2,1)} %reshape.156), calls=%async_computation.1 | async-start | bytes 1966080 | tf_op jit(solution)/shard_map/all_to_all | solution.py:64
  211.0 0.1 compare_convert_fusion
  211.1 0.1 broadcast_multiply_fusion.2
  211.1 0.0 all-gather.7.cloned.1.call-done
  211.1 2.2 reshape.155
  213.4 24.3 %all-to-all-done.1 = bf16[2,48,8,576]{3,2,0,1:T(8,128)(2,1)} async-done(((bf16[2,48,8,576]{3,2,0,1:T(8,128)(2,1)}), bf16[2,48,8,576]{3,2,0,1:T(8,128)(2,1)}, u32[]{:S(2)}, u32[]{:S(2)}) %all-to-all-start.1) | async-done | bytes 884768 | tf_op jit(solution)/shard_map/all_to_all | solution.py:64
  237.7 4.0 %fusion.6 = bf16[2,3,128,1152]{3,2,1,0:T(8,128)(2,1)} fusion(bf16[2,3,128,1152]{3,2,1,0:T(8,128)(2,1)S(1)} %copy-done.1, f32[2,3,1152]{2,1,0:T(4,128)S(1)} %broadcast_multiply_fusion.2, bf16[576,1152,1,1]{1,0,2,3:T(8,128)(2,1)S(1)} %reshape.155, bf16[2,3,16,8,576]{4,3,0,1,2:T(8,128)(2,1)} %bitcast.17), kind=kOutput, calls=%fused_computation.10 | convolution fusion | flops 1022754816 | bytes 5778432 | tf_op jit(solution)/shard_map/dot_general | solution.py:66
  (8 shorter events, 0.1 us)
Async XLA Ops:
  6.5 2.5 %copy-start.1 = (bf16[2,3,128,1152]{3,2,1,0:T(8,128)(2,1)S(1)}, bf16[2,3,128,1152]{3,2,1,0:T(8,128)(2,1)}, u32[]{:S(2)}) copy-start(bf16[2,3,128,1152]{3,2,1,0:T(8,128)(2,1)} %param.6) | copy-start | bytes 5308420
  6.5 3.1 %copy-start.4 = (f32[2,3,1152]{2,0,1:T(2,128)S(1)}, f32[2,3,1152]{2,0,1:T(2,128)}, u32[]{:S(2)}) copy-start(f32[2,3,1152]{2,0,1:T(2,128)} %param.7) | copy-start | bytes 82948
  6.5 53.4 %all-gather.5.cloned.1.call-start = ((), (), s32[]{:S(2)}) async-start(), calls=%async_computation.2 | async-start | bytes 4386816 | tf_op jit(solution)/shard_map/all_gather | solution.py:59
  82.8 5.3 %copy-start.5 = (s32[2,48]{1,0:T(2,128)S(1)}, s32[2,48]{1,0:T(2,128)}, u32[]{:S(2)}) copy-start(s32[2,48]{1,0:T(2,128)} %param.11) | copy-start | bytes 1156
  82.8 5.4 %copy-start.6 = (s32[2]{0:T(128)S(1)}, s32[2]{0:T(128)}, u32[]{:S(2)}) copy-start(s32[2]{0:T(128)} %param.10) | copy-start | bytes 28
  82.8 74.3 %all-to-all-start = ((bf16[2,3,128,1728]{3,0,1,2:T(2,128)(2,1)}), bf16[2,3,128,1728]{3,0,1,2:T(2,128)(2,1)}, u32[]{:S(2)}, u32[]{:S(2)}) async-start(bf16[2,3,128,1728]{3,0,1,2:T(2,128)(2,1)} %copy.54), calls=%async_computation | async-start | bytes 5505024 | tf_op jit(solution)/shard_map/all_to_all | solution.py:62
  87.4 123.7 %all-gather.7.cloned.1.call-start = ((), (), s32[]{:S(2)}) async-start(), calls=%async_computation.3 | async-start | bytes 1566720 | tf_op jit(solution)/shard_map/all_gather | solution.py:68
  193.1 3.8 %copy-start = (f32[2,48,8,1,8,72]{1,4,5,2,0,3:T(8,128)S(1)}, f32[2,48,8,1,8,72]{1,4,5,2,0,3:T(8,128)}, u32[]{:S(2)}) copy-start(f32[2,48,8,1,8,72]{1,4,5,2,0,3:T(8,128)} %copy.58) | copy-start | bytes 5308420
  196.9 0.8 copy-start.2
  196.9 0.8 copy-start.3
  198.9 1.1 copy-start.7
  205.6 32.1 %all-to-all-start.1 = ((bf16[2,48,8,576]{3,2,0,1:T(8,128)(2,1)}), bf16[2,48,8,576]{3,2,0,1:T(8,128)(2,1)}, u32[]{:S(2)}, u32[]{:S(2)}) async-start(bf16[2,48,8,576]{3,2,0,1:T(8,128)(2,1)} %reshape.156), calls=%async_computation.1 | async-start | bytes 1966080 | tf_op jit(solution)/shard_map/all_to_all | solution.py:64
Sparse Core Ops, SparseCore 0:
  9.5 50.4 all-gather.4
  90.4 66.4 all-gather.6
where the time goes:
time: 250 us; the launch traced here: 249 us
  waiting for transfers between devices  143 us (57%)
  local copies, waits for them, and re-layouts  46.8 us (19%)
  other arithmetic  21.2 us (8%)
  matrix products  14.4 us (6%)
  between operations  13.6 us (5%)
  starting transfers between devices  10 us (4%)
    all_to_all x1, waiting for transfers between devices, shards(): qkv = lax.all_to_all(qkv, 'seq', split_axis=2, concat_axis=1, tiled=True)  67.3 us
    all_gather x1, waiting for transfers between devices, shards(): lax.all_gather(w_qkv, 'seq', axis=1, tiled=True)  49.5 us
    all_to_all x1, waiting for transfers between devices, shards(): lax.all_to_all(attended, 'seq', split_axis=1, concat_axis=2, tiled=True)  24.3 us
    reshape x1, local copies, waits for them, and re-layouts, attend(): parts = qkv.reshape(clips, frames, patches, 3, H, HD)  8.79 us
    unnamed x18, local copies, waits for them, and re-layouts  8.44 us
    dot_general x1, matrix products, shards(): jnp.dot(flat, lax.all_gather(w_qkv, 'seq', axis=1, tiled=True), preferred...  7.29 us
    slice x1, other arithmetic, attend(): values = parts[:, :, :, 2]  6.16 us
    reshape x1, local copies, waits for them, and re-layouts, shards(): joined.astype(jnp.bfloat16)  6.15 us
  transfers between devices with their start and end apart: 4, of which 3 were waited for; matrix products, arithmetic and copies ran while one was open for 22% of the time, Pallas kernels for 0%

commit v1 on v0

v1 whole, which is shorter than its diff:
```python
import functools
import math

import jax
import jax.numpy as jnp
from jax import lax
from jax.experimental import pallas as pl
from jax.experimental.pallas import tpu as pltpu
from jax.sharding import PartitionSpec as P

MESH = pl.DeviceIdType.MESH
F32 = jnp.float32
BF16 = jnp.bfloat16

D = 1152
H = 8
HD = 72
C = 2
T = 48
SEQ = 16
NX = 4
NZ = 8
NY = 8
TL = 3
PL = 8
TOK = T * PL
HP = 80
QK = H * HP
KT = D // 128
ZREL = (0, 1, 7, 2, 6, 3, 5, 4)


def nt(a, b):
    return lax.dot_general(a, b, (((1,), (1,)), ((), ())), preferred_element_type=F32)


def nn(a, b):
    return lax.dot_general(a, b, (((1,), (0,)), ((), ())), preferred_element_type=F32)


def row_ids(shape):
    return lax.broadcasted_iota(jnp.int32, shape, 0)


def lane_ids(shape):
    return lax.broadcasted_iota(jnp.int32, shape, 1)


def normalise(xin, xm, mod_ref, c):
    @pl.loop(0, SEQ // 2)
    def _(k):
        v = xin[c, pl.ds(2 * k, 2)].astype(F32).reshape(2 * TL * PL, D)
        mean = jnp.mean(v, axis=-1, keepdims=True)
        v = v - mean
        var = jnp.mean(v * v, axis=-1, keepdims=True)
        normed = v * lax.rsqrt(var + 1e-6)
        shift = mod_ref[c, 0:1, :]
        scale = mod_ref[c, 1:2, :]
        rows = pl.ds(pl.multiple_of(48 * k, 48), 48)
        xm[c, rows, :] = (normed * (1.0 + scale) + shift).astype(BF16)


def tables(tp_ref, cf_ref, cos_t, even_t, odd_t, mask_t):
    shape = (HP, TOK)
    r = row_ids(shape)
    within = jnp.where(r >= 40, r - 40, r)
    feature = jnp.where(r >= 40, within + 36, within)
    pair = lax.shift_right_logical(feature, 1)
    freq = jnp.exp(pair.astype(F32) * (-math.log(10000.0) * 2.0 / HD))
    is_even = (r & 1) == 0
    frame = lax.shift_right_logical(lane_ids((8, TOK)), 3)
    key = row_ids((TOK, TOK))
    query = lane_ids((TOK, TOK))
    same = (key & 7) == (query & 7)
    key_frame = lax.shift_right_logical(key, 3)
    for c in range(C):
        pos = jnp.zeros((8, TOK), F32)
        for t in range(T):
            pos = jnp.where(frame == t, tp_ref[c, t].astype(F32), pos)
        angle = freq * pos[0:1]
        sine = jnp.sin(angle)
        cos_t[c] = jnp.cos(angle)
        even_t[c] = jnp.where(is_even, -sine, 0.0)
        odd_t[c] = jnp.where(is_even, 0.0, sine)
        live = same & (key_frame < cf_ref[c])
        mask_t[c] = jnp.where(live, 1.0, 0.0).astype(BF16)


def pack_weights(wq_ref, wo_ref, wloc):
    for i in range(64):
        d, j = divmod(i, 2)
        kt, rt = divmod(i, 7)
        if kt < KT and rt < 6:
            tile = wq_ref[16 * rt : 16 * rt + 16, 128 * kt : 128 * kt + 128]
        elif kt < KT:
            part = wq_ref[96:108, 128 * kt : 128 * kt + 128].astype(F32)
            tile = jnp.concatenate([part, jnp.zeros((4, 128), F32)], axis=0).astype(BF16)
        else:
            tile = jnp.zeros((16, 128), BF16)
        wloc[d // NZ, d % NZ, j] = tile
    for d in range(32):
        kt, rt = divmod(d, 3)
        if kt < KT and rt < 2:
            tile = wo_ref[16 * rt : 16 * rt + 16, 128 * kt : 128 * kt + 128]
        elif kt < KT:
            part = wo_ref[32:36, 128 * kt : 128 * kt + 128].astype(F32)
            tile = jnp.concatenate([part, jnp.zeros((12, 128), F32)], axis=0).astype(BF16)
        else:
            tile = jnp.zeros((16, 128), BF16)
        wloc[d // NZ, d % NZ, 2] = tile


def spread_rows(g, y, kt, core):
    tiles = []
    for i in range(7 * kt, 7 * kt + 7):
        d, j = divmod(i, 2)
        tiles.append(g[core, y, d // NZ, d % NZ, j].astype(F32))
    w = jnp.concatenate(tiles, axis=0)
    moved = pltpu.roll(w, 4, 0)
    r = row_ids((40, 128))
    first = jnp.where(r < 36, w[0:40], 0.0)
    second = jnp.where(r < 36, moved[40:80], 0.0)
    return [first, second, w[72:112]]


def unpack_qkv(g, wt):
    @pl.loop(0, NY)
    def _(y):
        for kt in range(KT):
            rows = spread_rows(g, y, kt, 0) + spread_rows(g, y, kt, 1)
            block = jnp.concatenate(rows, axis=0).astype(BF16)
            wt[pl.ds(pl.multiple_of(240 * y, 240), 240), 128 * kt : 128 * kt + 128] = block


def unpack_out(g, wot):
    @pl.loop(0, NY)
    def _(y):
        for kt in range(KT):
            rows = []
            for core in range(2):
                tiles = []
                for d in range(3 * kt, 3 * kt + 3):
                    tiles.append(g[core, y, d // NZ, d % NZ, 2].astype(F32))
                rows.append(jnp.concatenate(tiles, axis=0)[0:40])
            block = jnp.concatenate(rows, axis=0).astype(BF16)
            wot[pl.ds(pl.multiple_of(HP * y, HP), HP), 128 * kt : 128 * kt + 128] = block


def rotate(v, cos, even, odd):
    total = jnp.sum(v * v, axis=0, keepdims=True)
    v = v * lax.rsqrt(total * (1.0 / HD) + 1e-6)
    up = pltpu.roll(v, HP - 1, 0)
    down = pltpu.roll(v, 1, 0)
    return (v * cos + up * even + down * odd).astype(BF16)


def attend(c, xm, wt, qkv_t, att_t, back, cos_t, even_t, odd_t, mask_t):
    x = xm[c]
    for block in range(3):
        rows = slice(QK * block, QK * (block + 1))
        qkv_t[rows, :] = nt(wt[rows, :], x).astype(BF16)

    ones_row = jnp.where(row_ids((HP, 1)) == 36, 1.0, 0.0).astype(BF16)

    for h in range(H):
        rows = HP * h
        cos, even, odd = cos_t[c], even_t[c], odd_t[c]
        q = rotate(qkv_t[rows : rows + HP].astype(F32), cos, even, odd)
        k = rotate(qkv_t[QK + rows : QK + rows + HP].astype(F32), cos, even, odd)
        v = qkv_t[2 * QK + rows : 2 * QK + rows + HP] + ones_row
        s = nn(k.T, q)
        e = jnp.exp(s * (1.0 / math.sqrt(HD))).astype(BF16) * mask_t[c]
        o = nn(v, e)
        att_t[rows : rows + HP] = (o / o[36:37]).astype(BF16)
    for j in range(QK // 128):
        lanes = slice(128 * j, 128 * j + 128)
        part = att_t[lanes, :].astype(F32).T
        back[c, :, :, :, lanes] = part.reshape(SEQ, TL, PL, 128).astype(BF16)


def kernel(
    lat, mod_ref, wq_ref, wo_ref, cf_ref, tp_ref, out,
    xin, xm, wloc, g, wt, wot, qkv_t, att_t, back, got, held, outv, cos_t, even_t, odd_t, mask_t,
    a_s, a_r, z_s, z_r, x_s, x_r, cq_s, cq_r, co_s, co_r, f_s, f_r, r_s, r_r, own_sem, held_sem, out_sem,
):
    s_me = lax.axis_index("seq")
    d_me = lax.axis_index("dp")
    y, core = s_me // 2, s_me % 2
    z, x = d_me // NX, d_me % NX

    def seq_id(s):
        return (s, d_me)

    def plane_id(zz, xx):
        return (s_me, zz * NX + xx)

    right = plane_id(z, (x + 1) % NX)
    left = plane_id(z, (x + NX - 1) % NX)
    sibling = seq_id(s_me + 1 - 2 * core)

    def remote(src, dst, send, recv, to):
        return pltpu.make_async_remote_copy(
            src_ref=src, dst_ref=dst, send_sem=send, recv_sem=recv, device_id=to, device_id_type=MESH
        )

    barrier = pltpu.get_barrier_semaphore()
    for r in range(1, SEQ):
        pl.semaphore_signal(barrier, inc=1, device_id=seq_id((s_me + r) % SEQ), device_id_type=MESH)
    for r in range(1, NZ):
        pl.semaphore_signal(barrier, inc=1, device_id=plane_id((z + r) % NZ, x), device_id_type=MESH)
    pl.semaphore_signal(barrier, inc=1, device_id=right, device_id_type=MESH)
    pl.semaphore_signal(barrier, inc=1, device_id=left, device_id_type=MESH)

    own = [pltpu.make_async_copy(lat.at[c, :, s_me], xin.at[c, s_me], own_sem.at[c]) for c in range(C)]
    for c in range(C):
        own[c].start()
    hold = pltpu.make_async_copy(lat, held, held_sem)
    hold.start()
    pack_weights(wq_ref, wo_ref, wloc)
    g[core, y, x, z] = wloc[x, z]
    pl.semaphore_wait(barrier, SEQ - 1 + NZ - 1 + 2)

    def piece(r):
        yy = (y + r) % NY
        return remote(wloc.at[x, z], g.at[core, y, x, z], a_s.at[r], a_r.at[r], seq_id(2 * yy + core))

    for r in (1, 7, 2, 6, 3, 5, 4):
        piece(r).start()

    def forth(c, r):
        to = (s_me + r) % SEQ
        return remote(lat.at[c, :, to], xin.at[c, s_me], f_s.at[c, r], f_r.at[c, r], seq_id(to))

    for r in (1, 15, 2, 14, 3, 13, 4, 12, 5, 11, 6, 10, 7, 9, 8):
        forth(0, r).start()

    tiles = (slice(0, 2), slice(2, 3))

    def part(kind, core_of, xx, zz):
        return g.at[core_of, :, xx, zz, tiles[kind]]

    def z_copy(kind, r):
        to = plane_id((z + r) % NZ, x)
        mine = part(kind, core, x, z)
        return remote(mine, mine, z_s.at[kind, r], z_r.at[kind, r], to)

    def x_copy(kind, way, k, xx, zz, to):
        block = part(kind, core, xx, zz)
        return remote(block, block, x_s.at[kind, way, k], x_r.at[kind, way, k], to)

    def core_copy_q(xr, k):
        block = part(0, core, (x + xr) % NX, (z + ZREL[k]) % NZ)
        return remote(block, block, cq_s.at[xr, k], cq_r.at[xr, k], sibling)

    def core_copy_o(xr):
        block = g.at[core, :, (x + xr) % NX, :, tiles[1]]
        return remote(block, block, co_s.at[xr], co_r.at[xr], sibling)

    for r in (1, 7, 2, 6, 3, 5, 4):
        piece(r).wait_recv()
    for r in (1, 7, 2, 6, 3, 5, 4):
        z_copy(0, r).start()
    for r in (1, 15, 2, 14, 3, 13, 4, 12, 5, 11, 6, 10, 7, 9, 8):
        forth(1, r).start()
    for r in (1, 7, 2, 6, 3, 5, 4):
        z_copy(1, r).start()

    tables(tp_ref, cf_ref, cos_t, even_t, odd_t, mask_t)

    def from_z(kind):
        for k, rel in enumerate(ZREL):
            zz = (z + rel) % NZ
            if rel:
                z_copy(kind, (NZ - rel) % NZ).wait_recv()
            x_copy(kind, 0, k, x, zz, right).start()
            x_copy(kind, 1, k, x, zz, left).start()
            if kind == 0:
                core_copy_q(0, k).start()

    def from_x(kind):
        before, after, across = (x + NX - 1) % NX, (x + 1) % NX, (x + 2) % NX

        def crossed(k):
            zz = (z + ZREL[k]) % NZ
            x_copy(kind, 2, k, across, zz, right).wait_recv()
            if kind == 0:
                core_copy_q(2, k).start()

        for k, rel in enumerate(ZREL):
            zz = (z + rel) % NZ

            def first():
                x_copy(kind, 0, k, before, zz, right).wait_recv()
                if k % 2 == 0:
                    x_copy(kind, 2, k, before, zz, right).start()
                if kind == 0:
                    core_copy_q(3, k).start()

            def second():
                x_copy(kind, 1, k, after, zz, left).wait_recv()
                if k % 2 == 1:
                    x_copy(kind, 2, k, after, zz, left).start()
                if kind == 0:
                    core_copy_q(1, k).start()

            if k % 2 == 0:
                first()
                second()
            else:
                second()
                first()
            if k >= 2:
                crossed(k - 2)
        crossed(6)
        crossed(7)

    from_z(0)
    from_z(1)
    from_x(0)

    def arrived(c):
        own[c].wait()
        for r in range(1, SEQ):
            forth(c, r).wait_recv()

    def give_back(c, r):
        to = (s_me + r) % SEQ
        return remote(back.at[c, to], got.at[c, :, s_me], r_s.at[c, r], r_r.at[c, r], seq_id(to))

    def keep(c):
        return pltpu.make_async_copy(back.at[c, s_me], got.at[c, :, s_me], own_sem.at[c])

    def clip(c):
        attend(c, xm, wt, qkv_t, att_t, back, cos_t, even_t, odd_t, mask_t)
        keep(c).start()
        for r in (1, 15, 2, 14, 3, 13, 4, 12, 5, 11, 6, 10, 7, 9, 8):
            give_back(c, r).start()

    arrived(0)
    normalise(xin, xm, mod_ref, 0)
    for k in range(NZ):
        for xr in range(NX):
            core_copy_q(xr, k).wait_recv()
    unpack_qkv(g, wt)
    clip(0)

    from_x(1)
    for xr in range(NX):
        core_copy_o(xr).start()
    arrived(1)
    normalise(xin, xm, mod_ref, 1)
    clip(1)
    for xr in range(NX):
        core_copy_o(xr).wait_recv()
    unpack_out(g, wot)
    hold.wait()

    def out_copy(c, f):
        return pltpu.make_async_copy(outv.at[c, f], out.at[c, f], out_sem.at[c, f])

    for c in range(C):
        keep(c).wait()
        for r in range(1, SEQ):
            give_back(c, r).wait_recv()
        gate = mod_ref[c, 2:3, :]
        for f in range(TL):
            a = got[c, f].astype(F32).reshape(SEQ * PL, QK).astype(BF16)
            p = nn(a, wot[...])
            live = jnp.where(TL * s_me + f < cf_ref[c], 1.0, 0.0)
            res = held[c, f].astype(F32).reshape(SEQ * PL, D) + (live * gate) * p
            outv[c, f] = res.reshape(SEQ, PL, D).astype(BF16)
            out_copy(c, f).start()

    for r in range(1, NY):
        piece(r).wait_send()
    for c in range(C):
        for r in range(1, SEQ):
            forth(c, r).wait_send()
            give_back(c, r).wait_send()
    for kind in range(2):
        for r in range(1, NZ):
            z_copy(kind, r).wait_send()
        for way in range(3):
            for k in range(NZ):
                x_copy(kind, way, k, x, z, right).wait_send()
    for xr in range(NX):
        core_copy_o(xr).wait_send()
        for k in range(NZ):
            core_copy_q(xr, k).wait_send()
    for c in range(C):
        for f in range(TL):
            out_copy(c, f).wait()


def shards(latents, modulation, w_qkv, w_out, clip_frames, time_positions):
    vmem = pl.BlockSpec(memory_space=pltpu.VMEM)
    smem = pl.BlockSpec(memory_space=pltpu.SMEM)
    hbm = pl.BlockSpec(memory_space=pl.ANY)
    dma = pltpu.SemaphoreType.DMA
    grouped = latents.reshape(C, TL, SEQ, PL, D)
    out = pl.pallas_call(
        kernel,
        out_shape=jax.ShapeDtypeStruct(grouped.shape, BF16),
        in_specs=[hbm, vmem, vmem, vmem, smem, smem],
        out_specs=hbm,
        scratch_shapes=[
            pltpu.VMEM((C, SEQ, TL, PL, D), BF16),
            pltpu.VMEM((C, TOK, D), BF16),
            pltpu.VMEM((NX, NZ, 3, 16, 128), BF16),
            pltpu.VMEM((2, NY, NX, NZ, 3, 16, 128), BF16),
            pltpu.VMEM((3 * QK, D), BF16),
            pltpu.VMEM((QK, D), BF16),
            pltpu.VMEM((3 * QK, TOK), BF16),
            pltpu.VMEM((QK, TOK), BF16),
            pltpu.VMEM((C, SEQ, TL, PL, QK), BF16),
            pltpu.VMEM((C, TL, SEQ, PL, QK), BF16),
            pltpu.VMEM((C, TL, SEQ, PL, D), BF16),
            pltpu.VMEM((C, TL, SEQ, PL, D), BF16),
            pltpu.VMEM((C, HP, TOK), F32),
            pltpu.VMEM((C, HP, TOK), F32),
            pltpu.VMEM((C, HP, TOK), F32),
            pltpu.VMEM((C, TOK, TOK), BF16),
            dma((NY,)), dma((NY,)),
            dma((2, NZ)), dma((2, NZ)),
            dma((2, 3, NZ)), dma((2, 3, NZ)),
            dma((NX, NZ)), dma((NX, NZ)),
            dma((NX,)), dma((NX,)),
            dma((C, SEQ)), dma((C, SEQ)),
            dma((C, SEQ)), dma((C, SEQ)),
            dma((C,)), dma, dma((C, TL)),
        ],
        compiler_params=pltpu.CompilerParams(
            collective_id=0, has_side_effects=True, vmem_limit_bytes=56 * 1024 * 1024
        ),
        cost_estimate=pl.CostEstimate(flops=6 * 10**9, bytes_accessed=8 * 10**6, transcendentals=10**7),
    )(grouped, modulation, w_qkv.T, w_out, clip_frames, time_positions)
    return out.reshape(latents.shape)


def solution(mesh):
    return jax.shard_map(
        shards,
        mesh=mesh,
        in_specs=(
            P("dp", "seq", None, None),
            P("dp", None, None),
            P(None, "seq"),
            P("seq", None),
            P("dp"),
            P("dp", None),
        ),
        out_specs=P("dp", "seq", None, None),
        check_vma=False,
    )
```

time: 250 us -> 101 us (0.40)
  waiting for transfers between devices: 143 us -> 0 us
  Pallas kernels: 0 us -> 96.6 us
  local copies, waits for them, and re-layouts: 46.8 us -> 4.19 us
  other arithmetic: 21.2 us -> 0 us
  matrix products: 14.4 us -> 0 us
  between operations: 13.6 us -> 0.01 us
  starting transfers between devices: 10 us -> 0 us
    pallas_call x0 -> x1, Pallas kernels: none -> 96.6 us  [shards(): pl.pallas_call(kernel, out_shape=jax.ShapeDtypeStruct(grouped.shape, BF16...]
    all_to_all x2 -> x0, waiting for transfers between devices: 91.6 us -> none  [the longest x1 67.3 us: shards(): qkv = lax.all_to_all(qkv, 'seq', split_axis=2, concat_axis=1, tiled=True)]
    all_gather x2 -> x0, waiting for transfers between devices: 49.5 us -> none  [the longest x1 49.5 us: shards(): lax.all_gather(w_qkv, 'seq', axis=1, tiled=True)]
    reshape x4 -> x0, local copies, waits for them, and re-layouts: 17.3 us -> none  [the longest x1 8.79 us: attend(): parts = qkv.reshape(clips, frames, patches, 3, H, HD)]
    convert_element_type x3 -> x0, local copies, waits for them, and re-layouts: 15 us -> none  [the longest x1 5.24 us: attend(): parts[:, :, :, 0].astype(jnp.float32)]
    dot_general x4 -> x0, matrix products: 14.4 us -> none  [the longest x1 7.29 us: shards(): jnp.dot(flat, lax.all_gather(w_qkv, 'seq', axis=1, tiled=True), preferred...]
    all_to_all x2 -> x0, starting transfers between devices: 9.98 us -> none  [the longest x1 5.39 us: shards(): lax.all_to_all(attended, 'seq', split_axis=1, concat_axis=2, tiled=True)]
    reduce_sum x3 -> x0, other arithmetic: 6.92 us -> none  [the longest x1 4.53 us: rms_norm(): return vec * lax.rsqrt(jnp.mean(vec * vec, axis=-1, keepdims=True) + 1e-06)]
  transfers between devices with their start and end apart: 4 -> 0, of which waited for: 3 -> 0; matrix products, arithmetic and copies ran while one was open for 22% -> 0% of each run, Pallas kernels for 0% -> 0%
where the time goes in v1:
time: 101 us
  Pallas kernels  96.6 us (96%)
  local copies, waits for them, and re-layouts  4.19 us (4%)
    pallas_call x1, Pallas kernels, shards(): pl.pallas_call(kernel, out_shape=jax.ShapeDtypeStruct(grouped.shape, BF16...  96.6 us
    unnamed x2, local copies, waits for them, and re-layouts  4.19 us

profile of v1, /device:TPU:1, one launch (start us, length us, event | category | flops | bytes accessed | tf_op | source)
XLA Modules:
  0.0 100.8 jit_solution(18155447751299773431)
XLA Ops:
  0.0 1.4 %copy.7.mod_ref = f32[2,3,1152]{2,1,0:T(4,128)} copy(f32[2,3,1152]{2,0,1:T(2,128)} %param.7) | data formatting | bytes 55296 | tf_op args[1]
  1.4 96.6 %shard_map.64 = bf16[2,3,16,8,1152]{4,3,2,1,0:T(8,128)(2,1)} custom-call(bf16[2,3,16,8,1152]{4,3,2,1,0:T(8,128)(2,1)} %bitcast.4, f32[2,3,1152]{2,1,0:T(4,128)} %copy.7.mod_ref, bf16[108,1152]{1,0:T(8,128)(2,1)} %bitcast.5, bf16[36,1152]{1,0:T(8,128)(2,1)} %wo_ref.1, s32[2]{0:T(128)} %cf_ref.1, s32[2,48]{1,0:T(2,128)} %tp_ref.1), custom_call_target="tpu_custom_call" | custom-call | flops 6000000000 | bytes 8000000 | tf_op jit(solution)/shard_map/pallas_call | solution.py:401
  98.0 2.8 %copy.9 = bf16[2,3,128,1152]{3,2,1,0:T(8,128)(2,1)} copy(bf16[2,3,128,1152]{3,2,1,0:T(8,128)(2,1)} %bitcast.3) | data formatting | bytes 3538944

commit v2 on v1

v2 whole, which is shorter than its diff:
```python
import functools
import math

import jax
import jax.numpy as jnp
from jax import lax
from jax.experimental import pallas as pl
from jax.experimental.pallas import tpu as pltpu
from jax.sharding import PartitionSpec as P

MESH = pl.DeviceIdType.MESH
F32 = jnp.float32
BF16 = jnp.bfloat16

D = 1152
H = 8
HD = 72
C = 2
T = 48
SEQ = 16
NX = 4
NZ = 8
NY = 8
TL = 3
PL = 8
TOK = T * PL
HP = 80
QK = H * HP
VD = H * HD
BACK = 14
KT = D // 128
ZREL = (0, 1, 7, 2, 6, 3, 5, 4)


def nt(a, b):
    return lax.dot_general(a, b, (((1,), (1,)), ((), ())), preferred_element_type=F32)


def nn(a, b):
    return lax.dot_general(a, b, (((1,), (0,)), ((), ())), preferred_element_type=F32)


def row_ids(shape):
    return lax.broadcasted_iota(jnp.int32, shape, 0)


def lane_ids(shape):
    return lax.broadcasted_iota(jnp.int32, shape, 1)


def normalise(xin, xm, mod_ref, c):
    @pl.loop(0, SEQ // 2)
    def _(k):
        v = xin[c, pl.ds(2 * k, 2)].astype(F32).reshape(2 * TL * PL, D)
        mean = jnp.mean(v, axis=-1, keepdims=True)
        v = v - mean
        var = jnp.mean(v * v, axis=-1, keepdims=True)
        normed = v * lax.rsqrt(var + 1e-6)
        shift = mod_ref[0, c : c + 1, :]
        scale = mod_ref[1, c : c + 1, :]
        rows = pl.ds(pl.multiple_of(48 * k, 48), 48)
        xm[c, rows, :] = (normed * (1.0 + scale) + shift).astype(BF16)


def tables(tp_ref, cf_ref, cos_t, even_t, odd_t, mask_t):
    shape = (HP, TOK)
    r = row_ids(shape)
    pair = lax.shift_right_logical(r, 1)
    freq = jnp.exp(pair.astype(F32) * (-math.log(10000.0) * 2.0 / HD))
    is_even = (r & 1) == 0
    frame = lax.shift_right_logical(lane_ids((8, TOK)), 3)
    key = row_ids((TOK, TOK))
    query = lane_ids((TOK, TOK))
    same = (key & 7) == (query & 7)
    key_frame = lax.shift_right_logical(key, 3)
    for c in range(C):
        pos = jnp.zeros((8, TOK), F32)
        for t in range(T):
            pos = jnp.where(frame == t, tp_ref[c, t].astype(F32), pos)
        angle = freq * pos[0:1]
        sine = jnp.sin(angle)
        cos_t[c] = jnp.cos(angle)
        even_t[c] = jnp.where(is_even, -sine, 0.0)
        odd_t[c] = jnp.where(is_even, 0.0, sine)
        live = same & (key_frame < cf_ref[c])
        mask_t[c] = jnp.where(live, 1.0, 0.0).astype(BF16)


def pack_weights(wq_ref, wo_ref, wloc):
    for i in range(64):
        d, j = divmod(i, 2)
        kt, rt = divmod(i, 7)
        if kt < KT and rt < 6:
            tile = wq_ref[16 * rt : 16 * rt + 16, 128 * kt : 128 * kt + 128]
        elif kt < KT:
            part = wq_ref[96:108, 128 * kt : 128 * kt + 128].astype(F32)
            tile = jnp.concatenate([part, jnp.zeros((4, 128), F32)], axis=0).astype(BF16)
        else:
            tile = jnp.zeros((16, 128), BF16)
        wloc[d // NZ, d % NZ, j] = tile
    for d in range(32):
        kt, rt = divmod(d, 3)
        if kt < KT and rt < 2:
            tile = wo_ref[16 * rt : 16 * rt + 16, 128 * kt : 128 * kt + 128]
        elif kt < KT:
            part = wo_ref[32:36, 128 * kt : 128 * kt + 128].astype(F32)
            tile = jnp.concatenate([part, jnp.zeros((12, 128), F32)], axis=0).astype(BF16)
        else:
            tile = jnp.zeros((16, 128), BF16)
        wloc[d // NZ, d % NZ, 2] = tile


def join(first, second, rows):
    second = pltpu.roll(second, 4, 0)
    cut = rows - 4
    return jnp.concatenate([first[:cut], first[cut : cut + 8] + second[:8], second[8 : rows + 4]], axis=0)


def unpack_qkv(g, wt):
    @pl.loop(0, NY)
    def _(y):
        for kt in range(KT):
            shard = []
            for core in range(2):
                tiles = []
                for i in range(7 * kt, 7 * kt + 7):
                    d, j = divmod(i, 2)
                    tiles.append(g[core, y, d // NZ, d % NZ, j].astype(F32))
                shard.append(jnp.concatenate(tiles, axis=0))
            w = join(shard[0], shard[1], 108)
            gap = jnp.zeros((8, 128), F32)
            rows = [w[0:72], gap, w[72:144], gap, w[144:216], gap]
            block = jnp.concatenate(rows, axis=0).astype(BF16)
            wt[pl.ds(pl.multiple_of(240 * y, 240), 240), 128 * kt : 128 * kt + 128] = block


def unpack_out(go, wot):
    @pl.loop(0, NY // 2)
    def _(i):
        for kt in range(KT):
            rows = []
            for j in range(2):
                shard = []
                for core in range(2):
                    tiles = []
                    for d in range(3 * kt, 3 * kt + 3):
                        tiles.append(go[core, d // NZ, d % NZ, 2 * i + j].astype(F32))
                    shard.append(jnp.concatenate(tiles, axis=0))
                rows.append(join(shard[0], shard[1], 36))
            block = jnp.concatenate(rows, axis=0).astype(BF16)
            wot[pl.ds(pl.multiple_of(144 * i, 144), 144), 128 * kt : 128 * kt + 128] = block

    wot[VD : VD + 128] = jnp.zeros((128, D), BF16)
    wot[VD + 128 : VD + 192] = wot[VD - 64 : VD]


def rotate(v, cos, even, odd):
    total = jnp.sum(v * v, axis=0, keepdims=True)
    v = v * lax.rsqrt(total * (1.0 / HD) + 1e-6)
    up = pltpu.roll(v, HP - 1, 0)
    down = pltpu.roll(v, 1, 0)
    return (v * cos + up * even + down * odd).astype(BF16)


def attend(c, part, xm, wt, qkv_t, att_t, back, cos_t, even_t, odd_t, mask_t):
    x = xm[c]
    for block in range(3):
        first = QK * block + QK // 2 * part
        rows = slice(first, first + QK // 2)
        qkv_t[rows, :] = nt(wt[rows, :], x).astype(BF16)

    ones_row = jnp.where(row_ids((HP, 1)) == HD, 1.0, 0.0).astype(BF16)
    for h in range(4 * part, 4 * part + 4):
        rows = HP * h
        cos, even, odd = cos_t[c], even_t[c], odd_t[c]
        q = rotate(qkv_t[rows : rows + HP].astype(F32), cos, even, odd)
        k = rotate(qkv_t[QK + rows : QK + rows + HP].astype(F32), cos, even, odd)
        v = qkv_t[2 * QK + rows : 2 * QK + rows + HP] + ones_row
        s = nn(k.T, q)
        e = jnp.exp(s * (1.0 / math.sqrt(HD))).astype(BF16) * mask_t[c]
        o = nn(v, e)
        att_t[HD * h : HD * h + HD] = o[:HD] / o[HD : HD + 1]
    for j in (2 * part, 2 * part + 1):
        turned = att_t[128 * j : 128 * j + 128].T.reshape(SEQ, TL, PL, 128)
        back[c, :, 3 * j : 3 * j + 3] = turned.astype(BF16)
    if part:
        last = att_t[VD - 64 : VD]
        turned = jnp.concatenate([last, last], axis=0).T.reshape(SEQ, TL, PL, 128)
        lane = lax.broadcasted_iota(jnp.int32, (SEQ, PL, 128), 2)
        back[c, :, 12] = jnp.where(lane < 64, turned[:, 0], turned[:, 1]).astype(BF16)
        back[c, :, 13] = turned[:, 2].astype(BF16)


def kernel(
    lat, mod_in, wq_in, wo_in, cf_ref, tp_ref, out,
    mod_ref, wq_ref, wo_ref, xin, xm, wloc, g, go, wt, wot, qkv_t, att_t, back, got, held, outv, cos_t, even_t, odd_t, mask_t,
    a_s, a_r, z_s, z_r, x_s, x_r, cq_s, cq_r, oz_s, oz_r, ox_s, ox_r, co_s, co_r, f_s, f_r, r_s, r_r, own_sem, in_sem, held_sem, out_sem,
):
    s_me = lax.axis_index("seq")
    d_me = lax.axis_index("dp")
    y, core = s_me // 2, s_me % 2
    z, x = d_me // NX, d_me % NX

    def seq_id(s):
        return (s, d_me)

    def plane_id(zz, xx):
        return (s_me, zz * NX + xx)

    sibling = seq_id(s_me + 1 - 2 * core)

    def remote(src, dst, send, recv, to):
        return pltpu.make_async_remote_copy(
            src_ref=src, dst_ref=dst, send_sem=send, recv_sem=recv, device_id=to, device_id_type=MESH
        )

    barrier = pltpu.get_barrier_semaphore()
    for r in range(1, SEQ):
        pl.semaphore_signal(barrier, inc=1, device_id=seq_id((s_me + r) % SEQ), device_id_type=MESH)
    z_next = (plane_id((z + 1) % NZ, x), plane_id((z + NZ - 1) % NZ, x))
    x_next = (plane_id(z, (x + 1) % NX), plane_id(z, (x + NX - 1) % NX))
    for r in range(1, NZ):
        pl.semaphore_signal(barrier, inc=1, device_id=plane_id((z + r) % NZ, x), device_id_type=MESH)
    for r in range(1, NX):
        pl.semaphore_signal(barrier, inc=1, device_id=plane_id(z, (x + r) % NX), device_id_type=MESH)

    loads = [
        pltpu.make_async_copy(wq_in, wq_ref, in_sem.at[0]),
        pltpu.make_async_copy(wo_in, wo_ref, in_sem.at[1]),
        pltpu.make_async_copy(mod_in, mod_ref, in_sem.at[2]),
    ]
    for copy in loads:
        copy.start()
    own = [pltpu.make_async_copy(lat.at[c, :, s_me], xin.at[c, s_me], own_sem.at[c]) for c in range(C)]
    for c in range(C):
        own[c].start()
    hold = pltpu.make_async_copy(lat, held, held_sem)
    hold.start()
    for copy in loads[:2]:
        copy.wait()
    pack_weights(wq_ref, wo_ref, wloc)
    g[core, y, x, z] = wloc[x, z]
    pl.semaphore_wait(barrier, SEQ - 1 + NZ - 1 + NX - 1)

    def piece(r):
        yy = (y + r) % NY
        return remote(wloc.at[x, z], g.at[core, y, x, z], a_s.at[r], a_r.at[r], seq_id(2 * yy + core))

    for r in (1, 7, 2, 6, 3, 5, 4):
        piece(r).start()

    def forth(c, r):
        to = (s_me + r) % SEQ
        return remote(lat.at[c, :, to], xin.at[c, s_me], f_s.at[c, r], f_r.at[c, r], seq_id(to))

    for r in (1, 15, 2, 14, 3, 13, 4, 12, 5, 11, 6, 10, 7, 9, 8):
        forth(0, r).start()

    half = (slice(0, NY // 2), slice(NY // 2, NY))
    tiles = slice(0, 2)

    def z_copy(way, m):
        zz = (z + (NZ - m if way == 0 else m) + 1 - 2 * way) % NZ
        ys = half[way] if m == NZ // 2 else slice(None)
        block = g.at[core, ys, x, zz, tiles]
        return remote(block, block, z_s.at[way, m], z_r.at[way, m], z_next[way])

    def x_copy(way, k, behind):
        xx = (x + (NX - behind if way == 0 else behind) + 1 - 2 * way) % NX
        block = g.at[core, :, xx, (z + ZREL[k]) % NZ, tiles]
        n = 2 * (behind - 1) + way
        return remote(block, block, x_s.at[n, k], x_r.at[n, k], x_next[way])

    def core_copy(xr, k):
        block = g.at[core, :, (x + xr) % NX, (z + ZREL[k]) % NZ, tiles]
        return remote(block, block, cq_s.at[xr, k], cq_r.at[xr, k], sibling)

    def column(k):
        x_copy(0, k, 1).start()
        x_copy(1, k, 1).start()
        core_copy(0, k).start()

    def z_step(m):
        for way in range(2):
            z_copy(way, m).wait_recv()
            if m < NZ // 2:
                z_copy(way, m + 1).start()
                column(2 * m - way)
        if m == NZ // 2:
            column(7)

    def x_step(k):
        for way in (k % 2, 1 - k % 2):
            x_copy(way, k, 1).wait_recv()
            if way == k % 2:
                x_copy(way, k, 2).start()
            core_copy((3, 1)[way], k).start()

    def x_across(k):
        x_copy(k % 2, k, 2).wait_recv()
        core_copy(2, k).start()

    def oz_copy(r):
        mine = g.at[core, :, x, z, 2]
        return remote(mine, go.at[core, x, z], oz_s.at[r], oz_r.at[r], plane_id((z + r) % NZ, x))

    def ox_copy(r):
        block = go.at[core, x]
        return remote(block, block, ox_s.at[r], ox_r.at[r], plane_id(z, (x + r) % NX))

    def o_core_copy(xr):
        block = go.at[core, (x + xr) % NX]
        return remote(block, block, co_s.at[xr], co_r.at[xr], sibling)

    for r in (1, 7, 2, 6, 3, 5, 4):
        piece(r).wait_recv()
    for way in range(2):
        z_copy(way, 1).start()
    column(0)
    for r in (1, 15, 2, 14, 3, 13, 4, 12, 5, 11, 6, 10, 7, 9, 8):
        forth(1, r).start()
    tables(tp_ref, cf_ref, cos_t, even_t, odd_t, mask_t)

    steps = [(2.4 * m, z_step, m) for m in range(1, 5)]
    steps += [(2.6 + 2.1 * k, x_step, k) for k in range(NZ)]
    steps += [(5.0 + 2.1 * k, x_across, k) for k in range(NZ)]
    for _, step, at in sorted(steps, key=lambda e: e[0]):
        step(at)
        if step is z_step and at == 3:
            go[core, x, z] = g[core, :, x, z, 2]
            for r in (1, 7, 2, 6, 3, 5, 4):
                oz_copy(r).start()
    for r in range(1, NZ):
        oz_copy(r).wait_recv()
    for r in (1, 3, 2):
        ox_copy(r).start()
    o_core_copy(0).start()

    def arrived(c):
        own[c].wait()
        for r in range(1, SEQ):
            forth(c, r).wait_recv()

    parts = (slice(0, 6), slice(6, BACK))

    def give_back(c, part, r):
        to = (s_me + r) % SEQ
        return remote(
            back.at[c, to, parts[part]], got.at[c, s_me, parts[part]], r_s.at[c, part, r], r_r.at[c, part, r], seq_id(to)
        )

    def keep(c):
        return pltpu.make_async_copy(back.at[c, s_me], got.at[c, s_me], own_sem.at[c])

    def clip(c):
        for part in range(2):
            attend(c, part, xm, wt, qkv_t, att_t, back, cos_t, even_t, odd_t, mask_t)
            for r in (1, 15, 2, 14, 3, 13, 4, 12, 5, 11, 6, 10, 7, 9, 8):
                give_back(c, part, r).start()
        keep(c).start()

    arrived(0)
    loads[2].wait()
    normalise(xin, xm, mod_ref, 0)
    for k in range(NZ):
        for xr in range(NX):
            core_copy(xr, k).wait_recv()
    unpack_qkv(g, wt)

    clip(0)
    for r in (1, 3, 2):
        ox_copy(r).wait_recv()
        o_core_copy(NX - r).start()
    arrived(1)
    normalise(xin, xm, mod_ref, 1)
    clip(1)
    for xr in range(NX):
        o_core_copy(xr).wait_recv()
    unpack_out(go, wot)
    hold.wait()

    def out_copy(c, f):
        return pltpu.make_async_copy(outv.at[c, f], out.at[c, f], out_sem.at[c, f])

    for c in range(C):
        keep(c).wait()
        for part in range(2):
            for r in range(1, SEQ):
                give_back(c, part, r).wait_recv()
        gate = mod_ref[2, c : c + 1, :]
        for f in range(TL):
            lanes = [got[c, :, at].astype(F32).reshape(SEQ * PL, 128) for at in (f, 3 + f, 6 + f, 9 + f, 12 + f // 2)]
            if f == 1:
                a = jnp.concatenate(lanes[:4], axis=1).astype(BF16)
                p = nn(a, wot[:512]) + nn(lanes[4].astype(BF16), wot[VD + 64 : VD + 192])
            else:
                p = nn(jnp.concatenate(lanes, axis=1).astype(BF16), wot[: VD + 64])
            live = jnp.where(TL * s_me + f < cf_ref[c], 1.0, 0.0)
            res = held[c, f].astype(F32).reshape(SEQ * PL, D) + (live * gate) * p
            outv[c, f] = res.reshape(SEQ, PL, D).astype(BF16)
            out_copy(c, f).start()

    for r in range(1, NY):
        piece(r).wait_send()
    for c in range(C):
        for r in range(1, SEQ):
            forth(c, r).wait_send()
            for part in range(2):
                give_back(c, part, r).wait_send()
    for way in range(2):
        for m in range(1, NZ // 2 + 1):
            z_copy(way, m).wait_send()
        for k in range(NZ):
            x_copy(way, k, 1).wait_send()
    for k in range(NZ):
        x_copy(k % 2, k, 2).wait_send()
    for r in range(1, NZ):
        oz_copy(r).wait_send()
    for r in range(1, NX):
        ox_copy(r).wait_send()
    for xr in range(NX):
        o_core_copy(xr).wait_send()
        for k in range(NZ):
            core_copy(xr, k).wait_send()
    for c in range(C):
        for f in range(TL):
            out_copy(c, f).wait()


def shards(latents, modulation, w_qkv, w_out, clip_frames, time_positions):
    smem = pl.BlockSpec(memory_space=pltpu.SMEM)
    hbm = pl.BlockSpec(memory_space=pl.ANY)
    dma = pltpu.SemaphoreType.DMA
    grouped = latents.reshape(C, TL, SEQ, PL, D)
    out = pl.pallas_call(
        kernel,
        out_shape=jax.ShapeDtypeStruct(grouped.shape, BF16),
        in_specs=[hbm, hbm, hbm, hbm, smem, smem],
        out_specs=hbm,
        scratch_shapes=[
            pltpu.VMEM((3, C, D), F32),
            pltpu.VMEM((3 * VD // SEQ, D), BF16),
            pltpu.VMEM((VD // SEQ, D), BF16),
            pltpu.VMEM((C, SEQ, TL, PL, D), BF16),
            pltpu.VMEM((C, TOK, D), BF16),
            pltpu.VMEM((NX, NZ, 3, 16, 128), BF16),
            pltpu.VMEM((2, NY, NX, NZ, 3, 16, 128), BF16),
            pltpu.VMEM((2, NX, NZ, NY, 16, 128), BF16),
            pltpu.VMEM((3 * QK, D), BF16),
            pltpu.VMEM((VD + 192, D), BF16),
            pltpu.VMEM((3 * QK, TOK), BF16),
            pltpu.VMEM((VD, TOK), F32),
            pltpu.VMEM((C, SEQ, BACK, PL, 128), BF16),
            pltpu.VMEM((C, SEQ, BACK, PL, 128), BF16),
            pltpu.VMEM((C, TL, SEQ, PL, D), BF16),
            pltpu.VMEM((C, TL, SEQ, PL, D), BF16),
            pltpu.VMEM((C, HP, TOK), F32),
            pltpu.VMEM((C, HP, TOK), F32),
            pltpu.VMEM((C, HP, TOK), F32),
            pltpu.VMEM((C, TOK, TOK), BF16),
            dma((NY,)), dma((NY,)),
            dma((2, 5)), dma((2, 5)),
            dma((4, NZ)), dma((4, NZ)),
            dma((NX, NZ)), dma((NX, NZ)),
            dma((NZ,)), dma((NZ,)),
            dma((NX,)), dma((NX,)),
            dma((NX,)), dma((NX,)),
            dma((C, SEQ)), dma((C, SEQ)),
            dma((C, 2, SEQ)), dma((C, 2, SEQ)),
            dma((C,)), dma((3,)), dma, dma((C, TL)),
        ],
        compiler_params=pltpu.CompilerParams(
            collective_id=0, has_side_effects=True, vmem_limit_bytes=56 * 1024 * 1024
        ),
        cost_estimate=pl.CostEstimate(flops=6 * 10**9, bytes_accessed=8 * 10**6, transcendentals=10**7),
    )(grouped, modulation.transpose(1, 0, 2), w_qkv.T, w_out, clip_frames, time_positions)
    return out.reshape(latents.shape)


def solution(mesh):
    return jax.shard_map(
        shards,
        mesh=mesh,
        in_specs=(
            P("dp", "seq", None, None),
            P("dp", None, None),
            P(None, "seq"),
            P("seq", None),
            P("dp"),
            P("dp", None),
        ),
        out_specs=P("dp", "seq", None, None),
        check_vma=False,
    )
```

time: 101 us -> 86.3 us (0.85)
  Pallas kernels: 96.6 us -> 83.3 us
  local copies, waits for them, and re-layouts: 4.19 us -> 2.82 us
    pallas_call x1, Pallas kernels: 96.6 us -> 83.3 us  [shards(): pl.pallas_call(kernel, out_shape=jax.ShapeDtypeStruct(grouped.shape, BF16...]
    unnamed x2 -> x1, local copies, waits for them, and re-layouts: 4.19 us -> 2.82 us
where the time goes in v2:
time: 86.3 us; the launch traced here: 86.1 us
  Pallas kernels  83.3 us (97%)
  local copies, waits for them, and re-layouts  2.82 us (3%)
    pallas_call x1, Pallas kernels, shards(): pl.pallas_call(kernel, out_shape=jax.ShapeDtypeStruct(grouped.shape, BF16...  83.3 us
    unnamed x1, local copies, waits for them, and re-layouts  2.82 us

profile of v2, /device:TPU:1, one launch (start us, length us, event | category | flops | bytes accessed | tf_op | source)
XLA Modules:
  0.0 86.1 jit_solution(7615955339187029564)
XLA Ops:
  0.0 83.3 %shard_map.64 = bf16[2,3,16,8,1152]{4,3,2,1,0:T(8,128)(2,1)} custom-call(bf16[2,3,16,8,1152]{4,3,2,1,0:T(8,128)(2,1)} %bitcast.5, f32[3,2,1152]{2,1,0:T(2,128)} %bitcast.7, bf16[108,1152]{1,0:T(8,128)(2,1)} %bitcast.6, bf16[36,1152]{1,0:T(8,128)(2,1)} %wo_in.1, s32[2]{0:T(128)} %cf_ref.1, s32[2,48]{1,0:T(2,128)} %tp_ref.1), custom_call_target="tpu_custom_call" | custom-call | flops 6000000000 | bytes 8000000 | tf_op jit(solution)/shard_map/pallas_call | solution.py:435
  83.3 2.8 %copy.8 = bf16[2,3,128,1152]{3,2,1,0:T(8,128)(2,1)} copy(bf16[2,3,128,1152]{3,2,1,0:T(8,128)(2,1)} %bitcast.4) | data formatting | bytes 3538944

commit v3 on v2

--- a/solution.py
+++ b/solution.py
@@ -30,6 +30,9 @@
 BACK = 14
 KT = D // 128
 ZREL = (0, 1, 7, 2, 6, 3, 5, 4)
+NEAR_SEQ = (1, 15, 2, 14, 3, 13, 4, 12, 5, 11, 6, 10, 7, 9, 8)
+FAR_SEQ = NEAR_SEQ[::-1]
+NEAR_EIGHT = (1, 7, 2, 6, 3, 5, 4)
 
 
 def nt(a, b):
@@ -235,7 +238,6 @@
     for c in range(C):
         own[c].start()
     hold = pltpu.make_async_copy(lat, held, held_sem)
-    hold.start()
     for copy in loads[:2]:
         copy.wait()
     pack_weights(wq_ref, wo_ref, wloc)
@@ -246,14 +248,14 @@
         yy = (y + r) % NY
         return remote(wloc.at[x, z], g.at[core, y, x, z], a_s.at[r], a_r.at[r], seq_id(2 * yy + core))
 
-    for r in (1, 7, 2, 6, 3, 5, 4):
+    for r in NEAR_EIGHT:
         piece(r).start()
 
     def forth(c, r):
         to = (s_me + r) % SEQ
         return remote(lat.at[c, :, to], xin.at[c, s_me], f_s.at[c, r], f_r.at[c, r], seq_id(to))
 
-    for r in (1, 15, 2, 14, 3, 13, 4, 12, 5, 11, 6, 10, 7, 9, 8):
+    for r in NEAR_SEQ:
         forth(0, r).start()
 
     half = (slice(0, NY // 2), slice(NY // 2, NY))
@@ -312,12 +314,12 @@
         block = go.at[core, (x + xr) % NX]
         return remote(block, block, co_s.at[xr], co_r.at[xr], sibling)
 
-    for r in (1, 7, 2, 6, 3, 5, 4):
+    for r in NEAR_EIGHT:
         piece(r).wait_recv()
     for way in range(2):
         z_copy(way, 1).start()
     column(0)
-    for r in (1, 15, 2, 14, 3, 13, 4, 12, 5, 11, 6, 10, 7, 9, 8):
+    for r in NEAR_SEQ:
         forth(1, r).start()
     tables(tp_ref, cf_ref, cos_t, even_t, odd_t, mask_t)
 
@@ -328,7 +330,7 @@
         step(at)
         if step is z_step and at == 3:
             go[core, x, z] = g[core, :, x, z, 2]
-            for r in (1, 7, 2, 6, 3, 5, 4):
+            for r in NEAR_EIGHT:
                 oz_copy(r).start()
     for r in range(1, NZ):
         oz_copy(r).wait_recv()
@@ -355,7 +357,7 @@
     def clip(c):
         for part in range(2):
             attend(c, part, xm, wt, qkv_t, att_t, back, cos_t, even_t, odd_t, mask_t)
-            for r in (1, 15, 2, 14, 3, 13, 4, 12, 5, 11, 6, 10, 7, 9, 8):
+            for r in FAR_SEQ:
                 give_back(c, part, r).start()
         keep(c).start()
 
@@ -368,6 +370,7 @@
     unpack_qkv(g, wt)
 
     clip(0)
+    hold.start()
     for r in (1, 3, 2):
         ox_copy(r).wait_recv()
         o_core_copy(NX - r).start()
@@ -378,12 +381,35 @@
         o_core_copy(xr).wait_recv()
     unpack_out(go, wot)
     hold.wait()
+    for r in range(1, NY):
+        piece(r).wait_send()
+    for c in range(C):
+        for r in range(1, SEQ):
+            forth(c, r).wait_send()
+    for way in range(2):
+        for m in range(1, NZ // 2 + 1):
+            z_copy(way, m).wait_send()
+        for k in range(NZ):
+            x_copy(way, k, 1).wait_send()
+    for k in range(NZ):
+        x_copy(k % 2, k, 2).wait_send()
+    for r in range(1, NZ):
+        oz_copy(r).wait_send()
+    for r in range(1, NX):
+        ox_copy(r).wait_send()
+    for xr in range(NX):
+        o_core_copy(xr).wait_send()
+        for k in range(NZ):
+            core_copy(xr, k).wait_send()
 
     def out_copy(c, f):
         return pltpu.make_async_copy(outv.at[c, f], out.at[c, f], out_sem.at[c, f])
 
     for c in range(C):
         keep(c).wait()
+        for part in range(2):
+            for r in range(1, SEQ):
+                give_back(c, part, r).wait_send()
         for part in range(2):
             for r in range(1, SEQ):
                 give_back(c, part, r).wait_recv()
@@ -400,31 +426,22 @@
             outv[c, f] = res.reshape(SEQ, PL, D).astype(BF16)
             out_copy(c, f).start()
 
-    for r in range(1, NY):
-        piece(r).wait_send()
-    for c in range(C):
-        for r in range(1, SEQ):
-            forth(c, r).wait_send()
-            for part in range(2):
-                give_back(c, part, r).wait_send()
-    for way in range(2):
-        for m in range(1, NZ // 2 + 1):
-            z_copy(way, m).wait_send()
-        for k in range(NZ):
-            x_copy(way, k, 1).wait_send()
-    for k in range(NZ):
-        x_copy(k % 2, k, 2).wait_send()
-    for r in range(1, NZ):
-        oz_copy(r).wait_send()
-    for r in range(1, NX):
-        ox_copy(r).wait_send()
-    for xr in range(NX):
-        o_core_copy(xr).wait_send()
-        for k in range(NZ):
-            core_copy(xr, k).wait_send()
     for c in range(C):
         for f in range(TL):
             out_copy(c, f).wait()
+
+
+def hand_out(src, dst, buf, in_sem, out_sem):
+    blocks = [(c, f) for c in range(C) for f in range(TL)]
+    into = [pltpu.make_async_copy(src.at[at], buf.at[at], in_sem.at[at]) for at in blocks]
+    onto = [pltpu.make_async_copy(buf.at[at], dst.at[at], out_sem.at[at]) for at in blocks]
+    for copy in into:
+        copy.start()
+    for one, other in zip(into, onto):
+        one.wait()
+        other.start()
+    for copy in onto:
+        copy.wait()
 
 
 def shards(latents, modulation, w_qkv, w_out, clip_frames, time_positions):
@@ -474,6 +491,14 @@
         ),
         cost_estimate=pl.CostEstimate(flops=6 * 10**9, bytes_accessed=8 * 10**6, transcendentals=10**7),
     )(grouped, modulation.transpose(1, 0, 2), w_qkv.T, w_out, clip_frames, time_positions)
+    out = pl.pallas_call(
+        hand_out,
+        out_shape=jax.ShapeDtypeStruct(grouped.shape, BF16),
+        in_specs=[hbm],
+        out_specs=hbm,
+        scratch_shapes=[pltpu.VMEM(grouped.shape, BF16), dma((C, TL)), dma((C, TL))],
+        cost_estimate=pl.CostEstimate(flops=0, bytes_accessed=4 * 10**6, transcendentals=0),
+    )(out)
     return out.reshape(latents.shape)
 
 

time: 86.3 us -> 83.7 us (0.970)
  local copies, waits for them, and re-layouts: 2.82 us -> 0 us
    unnamed x1 -> x0, local copies, waits for them, and re-layouts: 2.82 us -> none
    pallas_call x1, Pallas kernels: 83.3 us -> 80.9 us  [shards(): pl.pallas_call(kernel, out_shape=jax.ShapeDtypeStruct(grouped.shape, BF16...]
    pallas_call x0 -> x1, Pallas kernels: none -> 2.27 us  [shards(): pl.pallas_call(hand_out, out_shape=jax.ShapeDtypeStruct(grouped.shape, BF...]
where the time goes in v3:
time: 83.7 us; the launch traced here: 83.3 us
  Pallas kernels  83.1 us (99%)
    pallas_call x1, Pallas kernels, shards(): pl.pallas_call(kernel, out_shape=jax.ShapeDtypeStruct(grouped.shape, BF16...  80.9 us
    pallas_call x1, Pallas kernels, shards(): pl.pallas_call(hand_out, out_shape=jax.ShapeDtypeStruct(grouped.shape, BF...  2.27 us

profile of v3, /device:TPU:1, one launch (start us, length us, event | category | flops | bytes accessed | tf_op | source)
XLA Modules:
  0.0 83.3 jit_solution(474924992063158889)
XLA Ops:
  0.0 80.9 %shard_map.64.src = bf16[2,3,16,8,1152]{4,3,2,1,0:T(8,128)(2,1)} custom-call(bf16[2,3,16,8,1152]{4,3,2,1,0:T(8,128)(2,1)} %bitcast.4, f32[3,2,1152]{2,1,0:T(2,128)} %bitcast.6, bf16[108,1152]{1,0:T(8,128)(2,1)} %bitcast.5, bf16[36,1152]{1,0:T(8,128)(2,1)} %wo_in.1, s32[2]{0:T(128)} %cf_ref.1, s32[2,48]{1,0:T(2,128)} %tp_ref.1), custom_call_target="tpu_custom_call" | custom-call | flops 6000000000 | bytes 8000000 | tf_op jit(solution)/shard_map/pallas_call | solution.py:452
  80.9 2.3 %shard_map.65 = bf16[2,3,16,8,1152]{4,3,2,1,0:T(8,128)(2,1)} custom-call(bf16[2,3,16,8,1152]{4,3,2,1,0:T(8,128)(2,1)} %shard_map.64.src), custom_call_target="tpu_custom_call" | custom-call | bytes 4000000 | tf_op jit(solution)/shard_map/pallas_call | solution.py:494

commit v4 on v3

--- a/solution.py
+++ b/solution.py
@@ -32,6 +32,7 @@
 ZREL = (0, 1, 7, 2, 6, 3, 5, 4)
 NEAR_SEQ = (1, 15, 2, 14, 3, 13, 4, 12, 5, 11, 6, 10, 7, 9, 8)
 FAR_SEQ = NEAR_SEQ[::-1]
+LATE = 5
 NEAR_EIGHT = (1, 7, 2, 6, 3, 5, 4)
 
 
@@ -277,9 +278,15 @@
         block = g.at[core, :, (x + xr) % NX, (z + ZREL[k]) % NZ, tiles]
         return remote(block, block, cq_s.at[xr, k], cq_r.at[xr, k], sibling)
 
+    def far(k):
+        block = g.at[core, :, x, (z + ZREL[k]) % NZ, tiles]
+        return remote(block, block, x_s.at[2 + k % 2, k], x_r.at[2 + k % 2, k], plane_id(z, (x + 2) % NX))
+
     def column(k):
         x_copy(0, k, 1).start()
         x_copy(1, k, 1).start()
+        if k >= LATE:
+            far(k).start()
         core_copy(0, k).start()
 
     def z_step(m):
@@ -294,7 +301,7 @@
     def x_step(k):
         for way in (k % 2, 1 - k % 2):
             x_copy(way, k, 1).wait_recv()
-            if way == k % 2:
+            if way == k % 2 and k < LATE:
                 x_copy(way, k, 2).start()
             core_copy((3, 1)[way], k).start()
 

time: 83.7 us -> 83.5 us (level)
  no operation moved by 1% of the time
where the time goes in v4:
time: 83.5 us; the launch traced here: 83.4 us
  Pallas kernels  83.2 us (100%)
    pallas_call x1, Pallas kernels, shards(): pl.pallas_call(kernel, out_shape=jax.ShapeDtypeStruct(grouped.shape, BF16...  80.9 us
    pallas_call x1, Pallas kernels, shards(): pl.pallas_call(hand_out, out_shape=jax.ShapeDtypeStruct(grouped.shape, BF...  2.27 us

profile of v4, /device:TPU:1, one launch (start us, length us, event | category | flops | bytes accessed | tf_op | source)
XLA Modules:
  0.0 83.4 jit_solution(5640790598292150248)
XLA Ops:
  0.0 80.9 %shard_map.64.src = bf16[2,3,16,8,1152]{4,3,2,1,0:T(8,128)(2,1)} custom-call(bf16[2,3,16,8,1152]{4,3,2,1,0:T(8,128)(2,1)} %bitcast.4, f32[3,2,1152]{2,1,0:T(2,128)} %bitcast.6, bf16[108,1152]{1,0:T(8,128)(2,1)} %bitcast.5, bf16[36,1152]{1,0:T(8,128)(2,1)} %wo_in.1, s32[2]{0:T(128)} %cf_ref.1, s32[2,48]{1,0:T(2,128)} %tp_ref.1), custom_call_target="tpu_custom_call" | custom-call | flops 6000000000 | bytes 8000000 | tf_op jit(solution)/shard_map/pallas_call | solution.py:459
  80.9 2.3 %shard_map.65 = bf16[2,3,16,8,1152]{4,3,2,1,0:T(8,128)(2,1)} custom-call(bf16[2,3,16,8,1152]{4,3,2,1,0:T(8,128)(2,1)} %shard_map.64.src), custom_call_target="tpu_custom_call" | custom-call | bytes 4000000 | tf_op jit(solution)/shard_map/pallas_call | solution.py:501
